TPU v7x, 32 devices: a whole 2x2x4 slice. The times are simulated.
32 devices in a mesh: runs: 2 (over y), tensor: 16 (over z, x, core).
Axes of the slice: x: 2, y: 2, z: 4, core: 2. Of those that a mesh axis runs over, the one named last changes fastest.
Arguments:
- activations: bfloat16 [64, 512, 28672], P('runs', None, 'tensor'), parts along dimension 0, may hold values from -6 to 6
- output_gradient_rows: bfloat16 [64, 512, 8192], P('runs', None, 'tensor'), parts along dimension 0, may hold values from -6 to 6
- factor_in: bfloat16 [32, 32, 28672], P('runs', None, 'tensor'), parts along dimension 0, may hold values from -0.015625 to 0.015625
- factor_out: bfloat16 [32, 32, 8192], P('runs', None, 'tensor'), parts along dimension 0, may hold values from -0.02734375 to 0.02734375
- list_counts: int32 [32], P('runs'), parts along dimension 0, may hold values from 1 to 4, 40 in all
- list_seqs: int32 [32, 4], P('runs'), parts along dimension 0, may hold values from 0 to 31
Outputs:
- scores: float32 [512, 128], P('tensor', 'runs'), parts along dimension 1
- totals: float32 [32], P('runs'), parts along dimension 0
There are 2 independent parts, one for each index of `runs`. A program takes and returns all parts, laid end to end along the dimension named above; each array names one. Nothing has to cross between parts.
Inputs may be any that keep to these rules, and one draw needn't show every extreme that they name: `list_counts`: each query lists 1 to 4 sequences, 40 in all; some query lists exactly 4. `list_seqs`: sequence ids; only the first list_counts[q] slots of query q are read.
All inputs are finite; a program needn't handle non-finite values.
Results may differ from a plain program's by a relative error of at most 0.0003.
Values sent between devices are 32-bit elements; how exact they have to be, the bound alone decides.
No kernel may reach another device: no remote copies, remote signals or barrier semaphores. Data moves between devices by JAX's collectives and lax.ppermute only.
A program may use at most 256 MiB of HBM per device.

v0:
```python
import jax
import jax.numpy as jnp
from jax import lax
from jax.sharding import PartitionSpec as P


def per_device(activations, output_gradient_rows, factor_in, factor_out, list_counts, list_seqs):
    seqs_here, seq_length, width_in = activations.shape
    query_gradient_rows, rank, _ = factor_in.shape
    width_out = output_gradient_rows.shape[2]
    max_list = list_seqs.shape[1]
    devices = lax.axis_size("tensor")
    token_row_block = seq_length // devices
    input_projection_matrix = factor_in.reshape(query_gradient_rows * rank, width_in)
    output_projection_matrix = factor_out.reshape(query_gradient_rows * rank, width_out)
    query_grid = jnp.broadcast_to(
        jnp.arange(query_gradient_rows, dtype=jnp.int32)[:, None], (query_gradient_rows, max_list)
    )
    slot_grid = jnp.broadcast_to(
        jnp.arange(max_list, dtype=jnp.int32)[None, :], (query_gradient_rows, max_list)
    )
    valid_flat = (slot_grid < list_counts[:, None]).reshape(-1)
    chosen = (list_seqs * query_gradient_rows + query_grid).reshape(-1)
    columns = chosen.shape[0]
    inner_factor_basis = jnp.einsum(
        "joi,xi->ojx", activations, input_projection_matrix, preferred_element_type=jnp.float32
    )
    outer_factor_basis = jnp.einsum(
        "joi,xi->ojx",
        output_gradient_rows,
        output_projection_matrix,
        preferred_element_type=jnp.float32,
    )
    inner_factor_basis = inner_factor_basis.reshape(
        lax.axis_size("tensor") * token_row_block, seqs_here * query_gradient_rows, rank
    )
    outer_factor_basis = outer_factor_basis.reshape(
        lax.axis_size("tensor") * token_row_block, seqs_here * query_gradient_rows, rank
    )
    picked = jnp.concatenate(
        (
            jnp.take(inner_factor_basis, chosen, axis=1),
            jnp.take(outer_factor_basis, chosen, axis=1),
        ),
        axis=2,
    )
    summed = lax.psum_scatter(
        picked.reshape(lax.axis_size("tensor") * token_row_block, columns * 2 * rank),
        "tensor",
        scatter_dimension=0,
        tiled=True,
    )
    summed = summed.reshape(token_row_block, columns, 2, rank)
    scores_raw = jnp.sum(summed[:, :, 0, :] * summed[:, :, 1, :], axis=2)
    scores = jnp.where(valid_flat[None, :], scores_raw, jnp.float32(0.0))
    local_sums = jnp.sum(
        scores.reshape(token_row_block, query_gradient_rows, max_list), axis=(0, 2)
    )
    summed_totals = lax.psum(local_sums, "tensor")
    totals = summed_totals / jnp.sqrt((seq_length * list_counts).astype(jnp.float32))
    return (scores, totals)


def solution(mesh):
    in_specs = (
        P("runs", None, "tensor"),
        P("runs", None, "tensor"),
        P("runs", None, "tensor"),
        P("runs", None, "tensor"),
        P("runs"),
        P("runs", None),
    )
    out_specs = (P("tensor", "runs"), P("runs"))
    return jax.shard_map(
        per_device, mesh=mesh, in_specs=in_specs, out_specs=out_specs, check_vma=False
    )
```

profile of v0, /device:TPU:0, one launch (start us, length us, event | category | flops | bytes accessed | tf_op | source)
XLA Modules:
  0.0 252.8 jit_solution(13788669172635880987)
XLA Ops:
  7.2 0.0 copy-start
  7.2 0.0 reduce-scatter.4.cloned.1.call-start
  7.2 0.8 iota_add_fusion
  8.0 0.1 copy.10
  8.1 0.1 reshape.59
  8.3 0.4 copy-done
  8.7 39.7 %fusion.2 = f32[512,32,512]{2,0,1:T(8,128)} fusion(bf16[512,1792,1]{1,0,2:T(8,128)(2,1)S(1)} %bitcast.23, bf16[32,512,1792]{2,1,0:T(8,128)(2,1)} %param.8), kind=kOutput, calls=%fused_computation.15 | convolution fusion | flops 30064771072 | bytes 94109696 | tf_op jit(solution)/shard_map/joi,xi->ojx/dot_general | solution.py:25
  48.3 0.0 copy-start.2
  48.3 5.0 %gather_fusion = f32[64,512,32]{1,2,0:T(8,128)} fusion(f32[512,512,32]{0,2,1:T(8,128)} %bitcast.27, s32[1024]{0:T(1024)S(1)} %pad_clamp_fusion), kind=kCustom, calls=%fused_computation.clone | custom fusion | bytes 8388864 | tf_op jit(solution)/shard_map/jit(_take)/gather | solution.py:42
  53.4 0.0 copy-done.2
  53.4 23.2 %fusion.3 = f32[512,32,512]{2,0,1:T(8,128)} fusion(bf16[512,512,1]{1,0,2:T(8,128)(2,1)S(1)} %bitcast.28, bf16[32,512,512]{2,1,0:T(8,128)(2,1)} %param.9), kind=kOutput, calls=%fused_computation.16 | convolution fusion | flops 8589934592 | bytes 50855936 | tf_op jit(solution)/shard_map/joi,xi->ojx/dot_general | solution.py:28
  76.5 4.9 %gather_fusion.1 = f32[64,512,32]{1,2,0:T(8,128)} fusion(f32[512,512,32]{0,2,1:T(8,128)} %bitcast.24, s32[1024]{0:T(1024)S(1)} %pad_clamp_fusion), kind=kCustom, calls=%fused_computation.1.clone | custom fusion | bytes 8388864 | tf_op jit(solution)/shard_map/jit(_take)/gather | solution.py:43
  81.5 4.8 %select_bitcast_fusion.1 = (f32[512,64,32]{0,2,1:T(8,128)S(1)}, f32[512,64,32]{0,2,1:T(8,128)S(1)}) fusion(f32[64,512,32]{1,2,0:T(8,128)} %gather_fusion, pred[64]{0:T(512)(128)(4,1)S(1)} %compare_and_fusion, f32[64,512,32]{1,2,0:T(8,128)} %gather_fusion.1), kind=kLoop, calls=%fused_computation.4 | loop fusion | flops 2097152 | bytes 16777280 | tf_op jit(solution)/shard_map/jit(_take)/select_n | solution.py:42
  86.2 4.3 %pad_maximum_fusion = f32[512,64,64]{0,2,1:T(8,128)} fusion(f32[512,64,32]{0,2,1:T(8,128)S(1)} %get-tuple-element.8, f32[512,64,32]{0,2,1:T(8,128)S(1)} %get-tuple-element.7), kind=kLoop, calls=%fused_computation.2 | loop fusion | flops 2097152 | bytes 16777216 | tf_op jit(solution)/shard_map/concatenate | solution.py:40
  90.6 0.0 copy-start.1
  90.6 9.1 %copy.12 = f32[512,4096]{1,0:T(8,128)} copy(f32[512,4096]{0,1:T(8,128)} %bitcast.25) | data formatting | bytes 16777216
  99.7 0.0 copy-start.3
  99.7 0.0 reduce-scatter.4.cloned.1.call-update
  99.7 0.6 copy-done.3
  100.3 0.1 iota_compare_fusion
  100.4 0.1 lt.25
  100.5 106.8 %reduce-scatter.4.cloned.1.call-done = f32[32,4096]{1,0:T(8,128)} async-done(((f32[512,4096]{1,0:T(8,128)}), f32[32,4096]{1,0:T(8,128)}) %reduce-scatter.4.cloned.1.call-update) | async-done | bytes 524304
  207.2 3.0 %copy.13 = f32[32,4096]{0,1:T(8,128)} copy(f32[32,4096]{1,0:T(8,128)} %reduce-scatter.4.cloned.1.call-done) | data formatting | bytes 1048576
  210.2 1.9 fusion
  212.1 0.2 fusion.1
  212.3 0.1 reduce_sum.27
  212.4 0.1 reduce_sum.28
  212.5 0.7 copy.11
  213.2 32.2 %psum.7 = f32[16]{0:T(128)S(1)} all-reduce(f32[16]{0:T(128)S(1)} %reduce_sum.28), channel_id=1, replica_groups=mesh['runs'=2,'tensor'=16] {'tensor'}, use_global_device_ids=true, to_apply=%region_4.6 | all-reduce | flops 16 | bytes 128 | tf_op jit(solution)/shard_map/psum | solution.py:59
  245.4 0.5 rsqrt_multiply_fusion
  245.9 0.0 copy-done.1
  (3 shorter events, 0.0 us)
Async XLA Ops:
  7.2 1.5 copy-start
  7.2 200.1 %reduce-scatter.4.cloned.1.call-start = ((), (), s32[]{:S(2)}) async-start(), calls=%async_computation.1 | async-start | bytes 8912896
  48.3 5.1 %copy-start.2 = (bf16[16,32,512]{2,1,0:T(8,128)(2,1)S(1)}, bf16[16,32,512]{2,1,0:T(8,128)(2,1)}, u32[]{:S(2)}) copy-start(bf16[16,32,512]{2,1,0:T(8,128)(2,1)} %param.11) | copy-start | bytes 1572868
  90.6 155.3 %copy-start.1 = (bf16[16,32,1792]{2,1,0:T(8,128)(2,1)S(1)}, bf16[16,32,1792]{2,1,0:T(8,128)(2,1)}, u32[]{:S(2)}) copy-start(bf16[16,32,1792]{2,1,0:T(8,128)(2,1)} %param.10) | copy-start | bytes 5505028
  99.7 0.7 copy-start.3
Sparse Core Ops, SparseCore 0:
  99.8 107.3 reduce-scatter.3
where the time goes:
time: 253 us
  waiting for transfers between devices  107 us (42%)
  matrix products  62.8 us (25%)
  blocking collectives  32.2 us (13%)
  local copies, waits for them, and re-layouts  24.2 us (10%)
  between operations  14.1 us (6%)
  other arithmetic  12.7 us (5%)
    unnamed x2, waiting for transfers between devices  107 us
    dot_general x1, matrix products, per_device(): jnp.einsum('joi,xi->ojx', activations, input_projection_matrix, preferred...  39.7 us
    psum x1, blocking collectives, per_device(): summed_totals = lax.psum(local_sums, 'tensor')  32.2 us
    dot_general x1, matrix products, per_device(): jnp.einsum('joi,xi->ojx', output_gradient_rows, output_projection_matrix,...  23.2 us
    unnamed x11, local copies, waits for them, and re-layouts  13.8 us
  transfers between devices with their start and end apart: 1, of which 1 were waited for; matrix products, arithmetic and copies ran while one was open for 0% of the time, Pallas kernels for 0%

commit v1 on v0

v1 whole, which is shorter than its diff:
```python
import functools

import jax
import jax.numpy as jnp
import numpy as np
from jax import lax
from jax.experimental import pallas as pl
from jax.experimental.pallas import tpu as pltpu
from jax.sharding import PartitionSpec as P

PAIRS = 40
GROUP = 8
CHUNKS = (2, 3)


def stage_bits(devices, core):
    count = devices.bit_length() - 1
    bits = list(range(count))
    if core and count > 2:
        bits[1], bits[2] = bits[2], bits[1]
    return bits


def stage_pairs(devices, stage):
    return [(i, i ^ (1 << stage_bits(devices, i & 1)[stage])) for i in range(devices)]


def block_order(devices):
    half = devices // 2
    table = np.zeros((devices, devices), np.int32)
    for me in range(devices):
        for part in range(2):
            owner = me ^ part
            bits = stage_bits(devices, owner & 1)[1:]
            for i in range(half):
                block = owner
                for position, bit in enumerate(reversed(bits)):
                    if i >> position & 1:
                        block ^= 1 << bit
                table[me, part * half + i] = block
    return table


def token_block(acc, block, rows):
    if rows % 8 == 0:
        return acc[pl.ds(pl.multiple_of(block * rows, rows), rows), :]
    share = 8 // rows
    tile = acc[pl.ds(pl.multiple_of(block // share * 8, 8), 8), :]
    found = tile[:rows]
    for i in range(1, share):
        found = jnp.where(lax.rem(block, share) == i, tile[i * rows : (i + 1) * rows], found)
    return found


def project_kernel(base, slots, max_list, rank, info, act, grad, fin, fout, keep, send, fin_g, fout_g, acc):
    step = pl.program_id(0)
    lane_pair = lax.rem(step, GROUP)
    width = GROUP * rank
    seq = info[base + step] // slots
    before = info[base + jnp.maximum(step - 1, 0)] // slots

    @pl.when(lane_pair == 0)
    def _():
        for j in range(GROUP):
            query = lax.rem(info[base + step + j], slots) // max_list
            fin_g[j * rank : (j + 1) * rank, :] = fin[query]
            fout_g[j * rank : (j + 1) * rank, :] = fout[query]

    @pl.when((lane_pair == 0) | (seq != before))
    def _():
        dims = (((1,), (1,)), ((), ()))
        inner = lax.dot_general(act[0], fin_g[...], dims, preferred_element_type=jnp.float32)
        outer = lax.dot_general(grad[0], fout_g[...], dims, preferred_element_type=jnp.float32)
        live = lax.broadcasted_iota(jnp.int32, inner.shape, 1) >= lane_pair * rank
        acc[:, :width] = jnp.where(live, inner, acc[:, :width])
        acc[:, width:] = jnp.where(live, outer, acc[:, width:])

    @pl.when(lane_pair == GROUP - 1)
    def _():
        blocks = info.shape[0] - PAIRS
        rows = acc.shape[0] // blocks
        for i in range(blocks // 2):
            keep[i * rows : (i + 1) * rows, :] = token_block(acc, info[PAIRS + i], rows)
            send[i * rows : (i + 1) * rows, :] = token_block(acc, info[PAIRS + blocks // 2 + i], rows)


def project(first_group, groups, info, activations, output_gradient_rows, factor_in, factor_out, max_list):
    _, tokens, width_in = activations.shape
    width_out = output_gradient_rows.shape[2]
    queries, rank, _ = factor_in.shape
    base = first_group * GROUP
    slots = queries * max_list
    columns = 2 * GROUP * rank

    def seq_block(step, info):
        return (info[base + step] // slots, 0, 0)

    out = jax.ShapeDtypeStruct((tokens // 2, groups * columns), jnp.float32)
    out_spec = pl.BlockSpec((tokens // 2, columns), lambda step, info: (0, step // GROUP))
    return pl.pallas_call(
        functools.partial(project_kernel, base, slots, max_list, rank),
        grid_spec=pltpu.PrefetchScalarGridSpec(
            num_scalar_prefetch=1,
            grid=(groups * GROUP,),
            in_specs=[
                pl.BlockSpec((1, tokens, width_in), seq_block),
                pl.BlockSpec((1, tokens, width_out), seq_block),
                pl.BlockSpec((queries, rank, width_in), lambda step, info: (0, 0, 0)),
                pl.BlockSpec((queries, rank, width_out), lambda step, info: (0, 0, 0)),
            ],
            out_specs=[out_spec, out_spec],
            scratch_shapes=[
                pltpu.VMEM((GROUP * rank, width_in), jnp.bfloat16),
                pltpu.VMEM((GROUP * rank, width_out), jnp.bfloat16),
                pltpu.VMEM((tokens, columns), jnp.float32),
            ],
        ),
        out_shape=[out, out],
        compiler_params=pltpu.CompilerParams(vmem_limit_bytes=40 * 1024 * 1024),
        name="project",
    )(info, activations, output_gradient_rows, factor_in, factor_out)


def per_device(activations, output_gradient_rows, factor_in, factor_out, list_counts, list_seqs):
    tokens = activations.shape[1]
    queries, rank, _ = factor_in.shape
    max_list = list_seqs.shape[1]
    devices = lax.axis_size("tensor")
    stages = devices.bit_length() - 1
    rows = tokens // devices
    slots = queries * max_list

    slot = jnp.arange(slots, dtype=jnp.int32)
    valid = (jnp.arange(max_list, dtype=jnp.int32)[None, :] < list_counts[:, None]).reshape(-1)
    key = jnp.where(valid, list_seqs.reshape(-1), activations.shape[0]) * slots + slot
    place = jnp.sum((key[None, :] < key[:, None]).astype(jnp.int32), axis=1)
    pair = jnp.arange(PAIRS, dtype=jnp.int32)
    ordered = jnp.sum(jnp.where(place[:, None] == pair[None, :], key[:, None], 0), axis=0)
    order = jnp.asarray(block_order(devices))[lax.axis_index("tensor")]
    info = jnp.concatenate([ordered, order])

    products = []
    first = 0
    for groups in CHUNKS:
        keep, send = project(
            first, groups, info, activations, output_gradient_rows, factor_in, factor_out, max_list
        )
        first += groups
        for stage in range(stages):
            got = lax.ppermute(send, "tensor", stage_pairs(devices, stage))
            if stage < stages - 1:
                half = keep.shape[0] // 2
                send = keep[half:] + got[half:]
                keep = keep[:half] + got[:half]
            else:
                keep = keep + got
        basis = keep.reshape(rows, groups, 2, GROUP * rank)
        products.append((basis[:, :, 0] * basis[:, :, 1]).reshape(rows, groups * GROUP * rank))
    product = jnp.concatenate(products, axis=1)
    slot_of = jnp.repeat(lax.rem(ordered, slots), rank)
    spread = (slot_of[:, None] == slot[None, :]).astype(jnp.float32)
    scores = jnp.dot(product, spread, precision=lax.Precision.HIGHEST)
    sums = jnp.sum(scores.reshape(rows, queries, max_list), axis=(0, 2))
    for stage in range(stages):
        sums = sums + lax.ppermute(sums, "tensor", stage_pairs(devices, stage))
    totals = sums / jnp.sqrt((tokens * list_counts).astype(jnp.float32))
    return (scores, totals)


def solution(mesh):
    in_specs = (
        P("runs", None, "tensor"),
        P("runs", None, "tensor"),
        P("runs", None, "tensor"),
        P("runs", None, "tensor"),
        P("runs"),
        P("runs", None),
    )
    out_specs = (P("tensor", "runs"), P("runs"))
    return jax.shard_map(
        per_device, mesh=mesh, in_specs=in_specs, out_specs=out_specs, check_vma=False
    )
```

time: 253 us -> 110 us (0.43)
  waiting for transfers between devices: 107 us -> 38 us
  matrix products: 62.8 us -> 1.05 us
  Pallas kernels: 0 us -> 48.8 us
  blocking collectives: 32.2 us -> 0 us
  local copies, waits for them, and re-layouts: 24.2 us -> 3.91 us
  starting transfers between devices: 0.04 us -> 16.3 us
  between operations: 14.1 us -> 0.76 us
  other arithmetic: 12.7 us -> 2.92 us
    unnamed x2 -> x0, waiting for transfers between devices: 107 us -> none
    dot_general x2 -> x1, matrix products: 62.8 us -> 1.05 us  [per_device(): scores = jnp.dot(product, spread, precision=lax.Precision.HIGHEST)]
    pallas_call x0 -> x2, Pallas kernels: none -> 48.8 us  [project(): pl.pallas_call(functools.partial(project_kernel, base, slots, max_list, r...]
    ppermute x0 -> x12, waiting for transfers between devices: none -> 38 us  [the longest x8 29.3 us: per_device(): got = lax.ppermute(send, 'tensor', stage_pairs(devices, stage))]
    psum x1 -> x0, blocking collectives: 32.2 us -> none  [per_device(): summed_totals = lax.psum(local_sums, 'tensor')]
    ppermute x0 -> x12, starting transfers between devices: none -> 16.3 us  [the longest x8 12.3 us: per_device(): got = lax.ppermute(send, 'tensor', stage_pairs(devices, stage))]
    unnamed x11 -> x8, local copies, waits for them, and re-layouts: 13.8 us -> 2.57 us
    gather x2 -> x0, local copies, waits for them, and re-layouts: 9.99 us -> none  [the longest x1 5.05 us: per_device(): jnp.take(inner_factor_basis, chosen, axis=1)]
  transfers between devices with their start and end apart: 1 -> 12, of which waited for: 1 -> 8; matrix products, arithmetic and copies ran while one was open for 0% -> 1% of each run, Pallas kernels for 0% -> 18%
where the time goes in v1:
time: 110 us; the launch traced here: 112 us
  Pallas kernels  48.8 us (44%)
  waiting for transfers between devices  38 us (35%)
  starting transfers between devices  16.3 us (15%)
  local copies, waits for them, and re-layouts  3.91 us (4%)
  other arithmetic  2.92 us (3%)
    pallas_call x2, Pallas kernels, project(): pl.pallas_call(functools.partial(project_kernel, base, slots, max_list, r...  48.8 us
    ppermute x8, waiting for transfers between devices, per_device(): got = lax.ppermute(send, 'tensor', stage_pairs(devices, stage))  29.3 us
    ppermute x8, starting transfers between devices, per_device(): got = lax.ppermute(send, 'tensor', stage_pairs(devices, stage))  12.3 us
    ppermute x4, waiting for transfers between devices, per_device(): sums = sums + lax.ppermute(sums, 'tensor', stage_pairs(devices, stage))  8.72 us
    ppermute x4, starting transfers between devices, per_device(): sums = sums + lax.ppermute(sums, 'tensor', stage_pairs(devices, stage))  3.98 us
    unnamed x8, local copies, waits for them, and re-layouts  2.57 us
  transfers between devices with their start and end apart: 12, of which 8 were waited for; matrix products, arithmetic and copies ran while one was open for 1% of the time, Pallas kernels for 18%

profile of v1, /device:TPU:0, one launch (start us, length us, event | category | flops | bytes accessed | tf_op | source)
XLA Modules:
  0.0 111.8 jit_solution(11981107168282024544)
XLA Ops:
  0.6 0.7 select_multiply_fusion
  1.3 0.1 copy.11
  1.4 0.1 mul.36
  1.5 0.2 convert_reduce_fusion
  1.7 0.1 select_reduce_fusion
  1.8 0.7 dynamic-slice_bitcast_fusion
  2.5 0.1 pad_add_fusion.info
  2.6 0.0 copy-start
  2.6 1.5 %copy-done = bf16[16,32,1792]{2,1,0:T(8,128)(2,1)S(1)} copy-done((bf16[16,32,1792]{2,1,0:T(8,128)(2,1)S(1)}, bf16[16,32,1792]{2,1,0:T(8,128)(2,1)}, u32[]{:S(2)}) %copy-start) | copy-done | bytes 1835032
  4.1 0.0 copy-start.1
  4.1 1.0 copy-done.1
  5.1 28.6 %project.3 = (f32[256,1536]{1,0:T(8,128)S(1)}, f32[256,1536]{1,0:T(8,128)S(1)}) custom-call(s32[56]{0:T(128)S(1)} %pad_add_fusion.info, bf16[32,512,1792]{2,1,0:T(8,128)(2,1)} %act.3, bf16[32,512,512]{2,1,0:T(8,128)(2,1)} %grad.3, bf16[16,32,1792]{2,1,0:T(8,128)(2,1)S(1)} %copy-done, bf16[16,32,512]{2,1,0:T(8,128)(2,1)S(1)} %copy-done.1), custom_call_target="tpu_custom_call" | custom-call | tf_op jit(solution)/shard_map/project/pallas_call | solution.py:100
  33.7 0.5 collective-permute-start.4
  34.2 20.3 %project.2 = (f32[256,1024]{1,0:T(8,128)S(1)}, f32[256,1024]{1,0:T(8,128)S(1)}) custom-call(s32[56]{0:T(128)S(1)} %pad_add_fusion.info, bf16[32,512,1792]{2,1,0:T(8,128)(2,1)} %act.3, bf16[32,512,512]{2,1,0:T(8,128)(2,1)} %grad.3, bf16[16,32,1792]{2,1,0:T(8,128)(2,1)S(1)} %copy-done, bf16[16,32,512]{2,1,0:T(8,128)(2,1)S(1)} %copy-done.1), custom_call_target="tpu_custom_call" | custom-call | tf_op jit(solution)/shard_map/project/pallas_call | solution.py:100
  54.5 0.1 collective-permute-start
  54.6 0.0 collective-permute-done.4
  54.6 0.3 slice_add_fusion.1
  54.9 3.0 %collective-permute-start.5 = (f32[128,1536]{1,0:T(8,128)S(1)}, f32[128,1536]{1,0:T(8,128)S(1)}, u32[]{:S(2)}, u32[]{:S(2)}) collective-permute-start(f32[128,1536]{1,0:T(8,128)S(1)} %get-tuple-element.11), channel_id=1, source_target_pairs={{0,2},{1,5},{2,0},{3,7},{4,6},{5,1},{6,4},{7,3},{8,10},{9,13},{10,... | collective-permute-start | bytes 2359304 | tf_op jit(solution)/shard_map/ppermute | solution.py:150
  57.9 0.0 collective-permute-done
  57.9 0.2 slice_add_fusion.3
  58.1 2.0 %collective-permute-start.1 = (f32[128,1024]{1,0:T(8,128)S(1)}, f32[128,1024]{1,0:T(8,128)S(1)}, u32[]{:S(2)}, u32[]{:S(2)}) collective-permute-start(f32[128,1024]{1,0:T(8,128)S(1)} %get-tuple-element.13), channel_id=1, source_target_pairs={{0,2},{1,5},{2,0},{3,7},{4,6},{5,1},{6,4},{7,3},{8,10},{9,13},{10,... | collective-permute-start | bytes 1572872 | tf_op jit(solution)/shard_map/ppermute | solution.py:150
  60.1 13.4 %collective-permute-done.1 = f32[128,1024]{1,0:T(8,128)S(1)} collective-permute-done((f32[128,1024]{1,0:T(8,128)S(1)}, f32[128,1024]{1,0:T(8,128)S(1)}, u32[]{:S(2)}, u32[]{:S(2)}) %collective-permute-start.1) | collective-permute-done | bytes 524320 | tf_op jit(solution)/shard_map/ppermute | solution.py:150
  73.5 0.1 slice_add_fusion.7
  73.5 2.1 %collective-permute-start.2 = (f32[64,1024]{1,0:T(8,128)S(1)}, f32[64,1024]{1,0:T(8,128)S(1)}, u32[]{:S(2)}, u32[]{:S(2)}) collective-permute-start(f32[64,1024]{1,0:T(8,128)S(1)} %get-tuple-element.17), channel_id=1, source_target_pairs={{0,4},{1,3},{2,6},{3,1},{4,0},{5,7},{6,2},{7,5},{8,12},{9,11},{10,... | collective-permute-start | bytes 786440 | tf_op jit(solution)/shard_map/ppermute | solution.py:150
  75.7 0.0 collective-permute-done.5
  75.7 0.1 slice_add_fusion.5
  75.8 0.1 collective-permute-start.6
  75.9 0.1 broadcast_in_dim.30
  76.0 0.1 eq.31
  76.0 4.0 %collective-permute-done.2 = f32[64,1024]{1,0:T(8,128)S(1)} collective-permute-done((f32[64,1024]{1,0:T(8,128)S(1)}, f32[64,1024]{1,0:T(8,128)S(1)}, u32[]{:S(2)}, u32[]{:S(2)}) %collective-permute-start.2) | collective-permute-done | bytes 262176 | tf_op jit(solution)/shard_map/ppermute | solution.py:150
  80.1 3.1 %collective-permute-start.3 = (f32[32,1024]{1,0:T(8,128)S(1)}, f32[32,1024]{1,0:T(8,128)S(1)}, u32[]{:S(2)}, u32[]{:S(2)}) collective-permute-start(f32[32,1024]{1,0:T(8,128)S(1)} %slice_add_fusion.10), channel_id=1, source_target_pairs={{0,8},{1,9},{2,10},{3,11},{4,12},{5,13},{6,14},{7,15},{8,0},{9,1},... | collective-permute-start | bytes 393224 | tf_op jit(solution)/shard_map/ppermute | solution.py:150
  83.2 4.7 %collective-permute-done.6 = f32[64,1536]{1,0:T(8,128)S(1)} collective-permute-done((f32[64,1536]{1,0:T(8,128)S(1)}, f32[64,1536]{1,0:T(8,128)S(1)}, u32[]{:S(2)}, u32[]{:S(2)}) %collective-permute-start.6) | collective-permute-done | bytes 393248 | tf_op jit(solution)/shard_map/ppermute | solution.py:150
  87.9 0.0 copy-start.2
  88.0 1.3 %collective-permute-start.7 = (f32[32,1536]{1,0:T(8,128)S(1)}, f32[32,1536]{1,0:T(8,128)S(1)}, u32[]{:S(2)}, u32[]{:S(2)}) collective-permute-start(f32[32,1536]{1,0:T(8,128)S(1)} %slice_add_fusion.8), channel_id=1, source_target_pairs={{0,8},{1,9},{2,10},{3,11},{4,12},{5,13},{6,14},{7,15},{8,0},{9,1},... | collective-permute-start | bytes 589832 | tf_op jit(solution)/shard_map/ppermute | solution.py:150
  89.3 0.0 collective-permute-done.3
  89.3 0.1 reshape.70
  89.4 0.2 fusion.8
  89.7 7.1 %collective-permute-done.7 = f32[32,1536]{1,0:T(8,128)S(1)} collective-permute-done((f32[32,1536]{1,0:T(8,128)S(1)}, f32[32,1536]{1,0:T(8,128)S(1)}, u32[]{:S(2)}, u32[]{:S(2)}) %collective-permute-start.7) | collective-permute-done | bytes 196640 | tf_op jit(solution)/shard_map/ppermute | solution.py:150
  96.8 0.1 reshape.71
  96.9 0.3 fusion.7
  97.3 1.1 fusion.11
  98.4 0.1 reduce_sum.37
  98.4 0.1 reduce_sum.38
  98.6 0.1 collective-permute-start.8
  98.6 1.1 collective-permute-done.8
  99.7 1.7 %collective-permute-start.9 = (f32[16]{0:T(128)S(1)}, f32[16]{0:T(128)S(1)}, u32[]{:S(2)}, u32[]{:S(2)}) collective-permute-start(f32[16]{0:T(128)S(1)} %add.84), channel_id=1, source_target_pairs={{0,2},{1,5},{2,0},{3,7},{4,6},{5,1},{6,4},{7,3},{8,10},{9,13},{10,... | collective-permute-start | bytes 200 | tf_op jit(solution)/shard_map/ppermute | solution.py:165
  101.4 1.9 %collective-permute-done.9 = f32[16]{0:T(128)S(1)} collective-permute-done((f32[16]{0:T(128)S(1)}, f32[16]{0:T(128)S(1)}, u32[]{:S(2)}, u32[]{:S(2)}) %collective-permute-start.9) | collective-permute-done | bytes 96 | tf_op jit(solution)/shard_map/ppermute | solution.py:165
  103.3 0.4 collective-permute-start.10
  103.7 3.1 %collective-permute-done.10 = f32[16]{0:T(128)S(1)} collective-permute-done((f32[16]{0:T(128)S(1)}, f32[16]{0:T(128)S(1)}, u32[]{:S(2)}, u32[]{:S(2)}) %collective-permute-start.10) | collective-permute-done | bytes 96 | tf_op jit(solution)/shard_map/ppermute | solution.py:165
  106.8 1.8 %collective-permute-start.11 = (f32[16]{0:T(128)S(1)}, f32[16]{0:T(128)S(1)}, u32[]{:S(2)}, u32[]{:S(2)}) collective-permute-start(f32[16]{0:T(128)S(1)} %add.86), channel_id=1, source_target_pairs={{0,8},{1,9},{2,10},{3,11},{4,12},{5,13},{6,14},{7,15},{8,0},{9,1},... | collective-permute-start | bytes 200 | tf_op jit(solution)/shard_map/ppermute | solution.py:165
  108.6 2.6 %collective-permute-done.11 = f32[16]{0:T(128)S(1)} collective-permute-done((f32[16]{0:T(128)S(1)}, f32[16]{0:T(128)S(1)}, u32[]{:S(2)}, u32[]{:S(2)}) %collective-permute-start.11) | collective-permute-done | bytes 96 | tf_op jit(solution)/shard_map/ppermute | solution.py:165
  111.3 0.0 copy-done.2
  111.3 0.5 rsqrt_multiply_fusion
  (11 shorter events, 0.1 us)
Async XLA Ops:
  2.6 1.5 %copy-start = (bf16[16,32,1792]{2,1,0:T(8,128)(2,1)S(1)}, bf16[16,32,1792]{2,1,0:T(8,128)(2,1)}, u32[]{:S(2)}) copy-start(bf16[16,32,1792]{2,1,0:T(8,128)(2,1)} %fin.3) | copy-start | bytes 5505028
  4.1 1.0 copy-start.1
  33.7 20.9 %collective-permute-start.4 = (f32[256,1536]{1,0:T(8,128)S(1)}, f32[256,1536]{1,0:T(8,128)S(1)}, u32[]{:S(2)}, u32[]{:S(2)}) collective-permute-start(f32[256,1536]{1,0:T(8,128)S(1)} %get-tuple-element.9), channel_id=1, source_target_pairs={{0,1},{1,0},{2,3},{3,2},{4,5},{5,4},{6,7},{7,6},{8,9},{9,8},{10,11... | collective-permute-start | bytes 4718600 | tf_op jit(solution)/shard_map/ppermute | solution.py:150
  54.5 3.4 %collective-permute-start = (f32[256,1024]{1,0:T(8,128)S(1)}, f32[256,1024]{1,0:T(8,128)S(1)}, u32[]{:S(2)}, u32[]{:S(2)}) collective-permute-start(f32[256,1024]{1,0:T(8,128)S(1)} %get-tuple-element.7), channel_id=1, source_target_pairs={{0,1},{1,0},{2,3},{3,2},{4,5},{5,4},{6,7},{7,6},{8,9},{9,8},{10,11... | collective-permute-start | bytes 3145736 | tf_op jit(solution)/shard_map/ppermute | solution.py:150
  54.9 20.8 %collective-permute-start.5 = (f32[128,1536]{1,0:T(8,128)S(1)}, f32[128,1536]{1,0:T(8,128)S(1)}, u32[]{:S(2)}, u32[]{:S(2)}) collective-permute-start(f32[128,1536]{1,0:T(8,128)S(1)} %get-tuple-element.11), channel_id=1, source_target_pairs={{0,2},{1,5},{2,0},{3,7},{4,6},{5,1},{6,4},{7,3},{8,10},{9,13},{10,... | collective-permute-start | bytes 2359304 | tf_op jit(solution)/shard_map/ppermute | solution.py:150
  58.1 15.4 %collective-permute-start.1 = (f32[128,1024]{1,0:T(8,128)S(1)}, f32[128,1024]{1,0:T(8,128)S(1)}, u32[]{:S(2)}, u32[]{:S(2)}) collective-permute-start(f32[128,1024]{1,0:T(8,128)S(1)} %get-tuple-element.13), channel_id=1, source_target_pairs={{0,2},{1,5},{2,0},{3,7},{4,6},{5,1},{6,4},{7,3},{8,10},{9,13},{10,... | collective-permute-start | bytes 1572872 | tf_op jit(solution)/shard_map/ppermute | solution.py:150
  73.5 6.5 %collective-permute-start.2 = (f32[64,1024]{1,0:T(8,128)S(1)}, f32[64,1024]{1,0:T(8,128)S(1)}, u32[]{:S(2)}, u32[]{:S(2)}) collective-permute-start(f32[64,1024]{1,0:T(8,128)S(1)} %get-tuple-element.17), channel_id=1, source_target_pairs={{0,4},{1,3},{2,6},{3,1},{4,0},{5,7},{6,2},{7,5},{8,12},{9,11},{10,... | collective-permute-start | bytes 786440 | tf_op jit(solution)/shard_map/ppermute | solution.py:150
  75.8 12.1 %collective-permute-start.6 = (f32[64,1536]{1,0:T(8,128)S(1)}, f32[64,1536]{1,0:T(8,128)S(1)}, u32[]{:S(2)}, u32[]{:S(2)}) collective-permute-start(f32[64,1536]{1,0:T(8,128)S(1)} %get-tuple-element.15), channel_id=1, source_target_pairs={{0,4},{1,3},{2,6},{3,1},{4,0},{5,7},{6,2},{7,5},{8,12},{9,11},{10,... | collective-permute-start | bytes 1179656 | tf_op jit(solution)/shard_map/ppermute | solution.py:150
  80.1 9.2 %collective-permute-start.3 = (f32[32,1024]{1,0:T(8,128)S(1)}, f32[32,1024]{1,0:T(8,128)S(1)}, u32[]{:S(2)}, u32[]{:S(2)}) collective-permute-start(f32[32,1024]{1,0:T(8,128)S(1)} %slice_add_fusion.10), channel_id=1, source_target_pairs={{0,8},{1,9},{2,10},{3,11},{4,12},{5,13},{6,14},{7,15},{8,0},{9,1},... | collective-permute-start | bytes 393224 | tf_op jit(solution)/shard_map/ppermute | solution.py:150
  87.9 23.3 %copy-start.2 = (s32[16]{0:T(128)S(1)}, s32[16]{0:T(128)}, u32[]{:S(2)}) copy-start(s32[16]{0:T(128)} %param.11) | copy-start | bytes 196
  88.0 8.8 %collective-permute-start.7 = (f32[32,1536]{1,0:T(8,128)S(1)}, f32[32,1536]{1,0:T(8,128)S(1)}, u32[]{:S(2)}, u32[]{:S(2)}) collective-permute-start(f32[32,1536]{1,0:T(8,128)S(1)} %slice_add_fusion.8), channel_id=1, source_target_pairs={{0,8},{1,9},{2,10},{3,11},{4,12},{5,13},{6,14},{7,15},{8,0},{9,1},... | collective-permute-start | bytes 589832 | tf_op jit(solution)/shard_map/ppermute | solution.py:150
  98.6 1.2 %collective-permute-start.8 = (f32[16]{0:T(128)S(1)}, f32[16]{0:T(128)S(1)}, u32[]{:S(2)}, u32[]{:S(2)}) collective-permute-start(f32[16]{0:T(128)S(1)} %reduce_sum.38), channel_id=1, source_target_pairs={{0,1},{1,0},{2,3},{3,2},{4,5},{5,4},{6,7},{7,6},{8,9},{9,8},{10,11... | collective-permute-start | bytes 200 | tf_op jit(solution)/shard_map/ppermute | solution.py:165
  99.7 3.5 %collective-permute-start.9 = (f32[16]{0:T(128)S(1)}, f32[16]{0:T(128)S(1)}, u32[]{:S(2)}, u32[]{:S(2)}) collective-permute-start(f32[16]{0:T(128)S(1)} %add.84), channel_id=1, source_target_pairs={{0,2},{1,5},{2,0},{3,7},{4,6},{5,1},{6,4},{7,3},{8,10},{9,13},{10,... | collective-permute-start | bytes 200 | tf_op jit(solution)/shard_map/ppermute | solution.py:165
  103.3 3.5 %collective-permute-start.10 = (f32[16]{0:T(128)S(1)}, f32[16]{0:T(128)S(1)}, u32[]{:S(2)}, u32[]{:S(2)}) collective-permute-start(f32[16]{0:T(128)S(1)} %add.85), channel_id=1, source_target_pairs={{0,4},{1,3},{2,6},{3,1},{4,0},{5,7},{6,2},{7,5},{8,12},{9,11},{10,... | collective-permute-start | bytes 200 | tf_op jit(solution)/shard_map/ppermute | solution.py:165
  106.8 4.4 %collective-permute-start.11 = (f32[16]{0:T(128)S(1)}, f32[16]{0:T(128)S(1)}, u32[]{:S(2)}, u32[]{:S(2)}) collective-permute-start(f32[16]{0:T(128)S(1)} %add.86), channel_id=1, source_target_pairs={{0,8},{1,9},{2,10},{3,11},{4,12},{5,13},{6,14},{7,15},{8,0},{9,1},... | collective-permute-start | bytes 200 | tf_op jit(solution)/shard_map/ppermute | solution.py:165

commit v2 on v1

--- a/solution.py
+++ b/solution.py
@@ -11,6 +11,7 @@
 PAIRS = 40
 GROUP = 8
 CHUNKS = (2, 3)
+BUFFERS = 4
 
 
 def stage_bits(devices, core):
@@ -52,73 +53,128 @@
     return found
 
 
-def project_kernel(base, slots, max_list, rank, info, act, grad, fin, fout, keep, send, fin_g, fout_g, acc):
-    step = pl.program_id(0)
-    lane_pair = lax.rem(step, GROUP)
-    width = GROUP * rank
-    seq = info[base + step] // slots
-    before = info[base + jnp.maximum(step - 1, 0)] // slots
-
-    @pl.when(lane_pair == 0)
-    def _():
-        for j in range(GROUP):
-            query = lax.rem(info[base + step + j], slots) // max_list
-            fin_g[j * rank : (j + 1) * rank, :] = fin[query]
-            fout_g[j * rank : (j + 1) * rank, :] = fout[query]
-
-    @pl.when((lane_pair == 0) | (seq != before))
-    def _():
-        dims = (((1,), (1,)), ((), ()))
-        inner = lax.dot_general(act[0], fin_g[...], dims, preferred_element_type=jnp.float32)
-        outer = lax.dot_general(grad[0], fout_g[...], dims, preferred_element_type=jnp.float32)
-        live = lax.broadcasted_iota(jnp.int32, inner.shape, 1) >= lane_pair * rank
-        acc[:, :width] = jnp.where(live, inner, acc[:, :width])
-        acc[:, width:] = jnp.where(live, outer, acc[:, width:])
-
-    @pl.when(lane_pair == GROUP - 1)
-    def _():
-        blocks = info.shape[0] - PAIRS
-        rows = acc.shape[0] // blocks
-        for i in range(blocks // 2):
-            keep[i * rows : (i + 1) * rows, :] = token_block(acc, info[PAIRS + i], rows)
-            send[i * rows : (i + 1) * rows, :] = token_block(acc, info[PAIRS + blocks // 2 + i], rows)
-
-
-def project(first_group, groups, info, activations, output_gradient_rows, factor_in, factor_out, max_list):
+def project_kernel(base, info, act, grad, fin, fout, keep, send, *scratch):
+    acts, grads, fins, fouts, acc, todo, act_sem, grad_sem, fin_sem, fout_sem = scratch
+    rank = fins.shape[2]
+    buffers = acts.shape[0]
+    tokens, columns = acc.shape
+    width = columns // 2
+    pairs = keep.shape[1] // columns * GROUP
+    blocks = info.shape[0] - 2 * PAIRS
+    rows = tokens // blocks
+
+    def is_new(pair):
+        return (pair == 0) | (info[base + pair] != info[base + jnp.maximum(pair - 1, 0)])
+
+    def list_new(pair, count):
+        new = is_new(pair)
+
+        @pl.when(new)
+        def _():
+            todo[count] = info[base + pair]
+
+        return count + new.astype(jnp.int32)
+
+    def sequence_copies(index):
+        buffer = lax.rem(index, buffers)
+        return (
+            pltpu.make_async_copy(act.at[todo[index]], acts.at[buffer], act_sem.at[buffer]),
+            pltpu.make_async_copy(grad.at[todo[index]], grads.at[buffer], grad_sem.at[buffer]),
+        )
+
+    def fetch_sequence(index):
+        for copy in sequence_copies(index):
+            copy.start()
+
+    def fetch_factors(group):
+        half = lax.rem(group, 2)
+        for i in range(GROUP):
+            query = info[PAIRS + base + group * GROUP + i]
+            pltpu.make_async_copy(fin.at[query], fins.at[half, i], fin_sem.at[half]).start()
+            pltpu.make_async_copy(fout.at[query], fouts.at[half, i], fout_sem.at[half]).start()
+
+    def wait_factors(group):
+        half = lax.rem(group, 2)
+        pltpu.make_async_copy(fin.at[pl.ds(0, GROUP)], fins.at[half], fin_sem.at[half]).wait()
+        pltpu.make_async_copy(fout.at[pl.ds(0, GROUP)], fouts.at[half], fout_sem.at[half]).wait()
+
+    fetch_factors(0)
+    count = lax.fori_loop(0, pairs, list_new, 0)
+    for i in range(buffers - 1):
+        pl.when(i < count)(functools.partial(fetch_sequence, i))
+
+    def one_pair(pair, index):
+        lane_pair = lax.rem(pair, GROUP)
+        group = pair // GROUP
+        half = lax.rem(group, 2)
+        new = is_new(pair)
+        index = index + new.astype(jnp.int32)
+        buffer = lax.rem(index, buffers)
+
+        @pl.when(lane_pair == 0)
+        def _():
+            wait_factors(group)
+            pl.when(group + 1 < pairs // GROUP)(lambda: fetch_factors(group + 1))
+
+        @pl.when(new)
+        def _():
+            for copy in sequence_copies(index):
+                copy.wait()
+            pl.when(index + buffers - 1 < count)(lambda: fetch_sequence(index + buffers - 1))
+
+        @pl.when((lane_pair == 0) | new)
+        def _():
+            dims = (((1,), (1,)), ((), ()))
+            live = lax.broadcasted_iota(jnp.int32, (tokens, width), 1) >= lane_pair * rank
+            for x, factors, lanes in ((acts, fins, slice(0, width)), (grads, fouts, slice(width, columns))):
+                basis = lax.dot_general(
+                    x[buffer],
+                    factors[half].reshape(width, factors.shape[3]),
+                    dims,
+                    preferred_element_type=jnp.float32,
+                )
+                acc[:, lanes] = jnp.where(live, basis, acc[:, lanes])
+
+        @pl.when(lane_pair == GROUP - 1)
+        def _():
+            lanes = pl.ds(pl.multiple_of(group * columns, columns), columns)
+            for i in range(blocks // 2):
+                here = slice(i * rows, (i + 1) * rows)
+                keep[here, lanes] = token_block(acc, info[2 * PAIRS + i], rows)
+                send[here, lanes] = token_block(acc, info[2 * PAIRS + blocks // 2 + i], rows)
+
+        return index
+
+    lax.fori_loop(0, pairs, one_pair, -1)
+
+
+def project(first_group, groups, info, activations, output_gradient_rows, factor_in, factor_out):
     _, tokens, width_in = activations.shape
     width_out = output_gradient_rows.shape[2]
-    queries, rank, _ = factor_in.shape
-    base = first_group * GROUP
-    slots = queries * max_list
+    rank = factor_in.shape[1]
+    arrays = (activations, output_gradient_rows, factor_in, factor_out)
     columns = 2 * GROUP * rank
-
-    def seq_block(step, info):
-        return (info[base + step] // slots, 0, 0)
-
     out = jax.ShapeDtypeStruct((tokens // 2, groups * columns), jnp.float32)
-    out_spec = pl.BlockSpec((tokens // 2, columns), lambda step, info: (0, step // GROUP))
     return pl.pallas_call(
-        functools.partial(project_kernel, base, slots, max_list, rank),
-        grid_spec=pltpu.PrefetchScalarGridSpec(
-            num_scalar_prefetch=1,
-            grid=(groups * GROUP,),
-            in_specs=[
-                pl.BlockSpec((1, tokens, width_in), seq_block),
-                pl.BlockSpec((1, tokens, width_out), seq_block),
-                pl.BlockSpec((queries, rank, width_in), lambda step, info: (0, 0, 0)),
-                pl.BlockSpec((queries, rank, width_out), lambda step, info: (0, 0, 0)),
-            ],
-            out_specs=[out_spec, out_spec],
-            scratch_shapes=[
-                pltpu.VMEM((GROUP * rank, width_in), jnp.bfloat16),
-                pltpu.VMEM((GROUP * rank, width_out), jnp.bfloat16),
-                pltpu.VMEM((tokens, columns), jnp.float32),
-            ],
-        ),
+        functools.partial(project_kernel, first_group * GROUP),
+        in_specs=[pl.BlockSpec(memory_space=pltpu.SMEM)] + [pl.BlockSpec(memory_space=pltpu.HBM)] * 4,
+        out_specs=[pl.BlockSpec(memory_space=pltpu.VMEM)] * 2,
+        scratch_shapes=[
+            pltpu.VMEM((BUFFERS, tokens, width_in), jnp.bfloat16),
+            pltpu.VMEM((BUFFERS, tokens, width_out), jnp.bfloat16),
+            pltpu.VMEM((2, GROUP, rank, width_in), jnp.bfloat16),
+            pltpu.VMEM((2, GROUP, rank, width_out), jnp.bfloat16),
+            pltpu.VMEM((tokens, columns), jnp.float32),
+            pltpu.SMEM((PAIRS,), jnp.int32),
+            pltpu.SemaphoreType.DMA((BUFFERS,)),
+            pltpu.SemaphoreType.DMA((BUFFERS,)),
+            pltpu.SemaphoreType.DMA((2,)),
+            pltpu.SemaphoreType.DMA((2,)),
+        ],
         out_shape=[out, out],
-        compiler_params=pltpu.CompilerParams(vmem_limit_bytes=40 * 1024 * 1024),
+        compiler_params=pltpu.CompilerParams(vmem_limit_bytes=24 * 1024 * 1024),
         name="project",
-    )(info, activations, output_gradient_rows, factor_in, factor_out)
+    )(info, *[pltpu.with_memory_space_constraint(x, pltpu.HBM) for x in arrays])
 
 
 def per_device(activations, output_gradient_rows, factor_in, factor_out, list_counts, list_seqs):
@@ -137,13 +193,13 @@
     pair = jnp.arange(PAIRS, dtype=jnp.int32)
     ordered = jnp.sum(jnp.where(place[:, None] == pair[None, :], key[:, None], 0), axis=0)
     order = jnp.asarray(block_order(devices))[lax.axis_index("tensor")]
-    info = jnp.concatenate([ordered, order])
+    info = jnp.concatenate([ordered // slots, lax.rem(ordered, slots) // max_list, order])
 
     products = []
     first = 0
     for groups in CHUNKS:
         keep, send = project(
-            first, groups, info, activations, output_gradient_rows, factor_in, factor_out, max_list
+            first, groups, info, activations, output_gradient_rows, factor_in, factor_out
         )
         first += groups
         for stage in range(stages):

time: 110 us -> 88.7 us (0.81); the launches traced: 112 us -> 87.3 us
  Pallas kernels: 48.8 us -> 26.9 us
  local copies, waits for them, and re-layouts: 3.91 us -> 1.37 us
    pallas_call x2, Pallas kernels: 48.8 us -> 26.9 us  [project(): pl.pallas_call(functools.partial(project_kernel, first_group * GROUP), in...]
    unnamed x8 -> x4, local copies, waits for them, and re-layouts: 2.57 us -> 0.03 us
  transfers between devices with their start and end apart: 12 -> 12, of which waited for: 8 -> 8; matrix products, arithmetic and copies ran while one was open for 1% -> 1% of each run, Pallas kernels for 18% -> 12%
where the time goes in v2:
time: 88.7 us; the launch traced here: 87.3 us
  waiting for transfers between devices  38.1 us (43%)
  Pallas kernels  26.9 us (30%)
  starting transfers between devices  16.2 us (18%)
  other arithmetic  2.93 us (3%)
  local copies, waits for them, and re-layouts  1.37 us (2%)
  matrix products  1.05 us (1%)
    ppermute x8, waiting for transfers between devices, per_device(): got = lax.ppermute(send, 'tensor', stage_pairs(devices, stage))  29.3 us
    pallas_call x2, Pallas kernels, project(): pl.pallas_call(functools.partial(project_kernel, first_group * GROUP), in...  26.9 us
    ppermute x8, starting transfers between devices, per_device(): got = lax.ppermute(send, 'tensor', stage_pairs(devices, stage))  12.3 us
    ppermute x4, waiting for transfers between devices, per_device(): sums = sums + lax.ppermute(sums, 'tensor', stage_pairs(devices, stage))  8.77 us
    ppermute x4, starting transfers between devices, per_device(): sums = sums + lax.ppermute(sums, 'tensor', stage_pairs(devices, stage))  3.93 us
  transfers between devices with their start and end apart: 12, of which 8 were waited for; matrix products, arithmetic and copies ran while one was open for 1% of the time, Pallas kernels for 12%

profile of v2, /device:TPU:0, one launch (start us, length us, event | category | flops | bytes accessed | tf_op | source)
XLA Modules:
  0.0 87.3 jit_solution(1500050276522988580)
XLA Ops:
  0.6 0.7 select_multiply_fusion
  1.3 0.1 copy.11
  1.4 0.1 mul.36
  1.5 0.2 convert_reduce_fusion
  1.7 0.1 select_reduce_fusion
  1.8 0.7 dynamic-slice_bitcast_fusion
  2.5 0.1 pad_add_fusion.info
  2.6 16.3 %project.3 = (f32[256,1536]{1,0:T(8,128)S(1)}, f32[256,1536]{1,0:T(8,128)S(1)}) custom-call(s32[96]{0:T(128)S(1)} %pad_add_fusion.info, bf16[32,512,1792]{2,1,0:T(8,128)(2,1)} %act.3, bf16[32,512,512]{2,1,0:T(8,128)(2,1)} %grad.3, bf16[16,32,1792]{2,1,0:T(8,128)(2,1)} %fin.3, bf16[16,32,512]{2,1,0:T(8,128)(2,1)} %fout.3), custom_call_target="tpu_custom_call" | custom-call | tf_op jit(solution)/shard_map/project/pallas_call | solution.py:158
  19.0 0.5 collective-permute-start.4
  19.5 10.5 %project.2 = (f32[256,1024]{1,0:T(8,128)S(1)}, f32[256,1024]{1,0:T(8,128)S(1)}) custom-call(s32[96]{0:T(128)S(1)} %pad_add_fusion.info, bf16[32,512,1792]{2,1,0:T(8,128)(2,1)} %act.3, bf16[32,512,512]{2,1,0:T(8,128)(2,1)} %grad.3, bf16[16,32,1792]{2,1,0:T(8,128)(2,1)} %fin.3, bf16[16,32,512]{2,1,0:T(8,128)(2,1)} %fout.3), custom_call_target="tpu_custom_call" | custom-call | tf_op jit(solution)/shard_map/project/pallas_call | solution.py:158
  30.0 0.1 collective-permute-start
  30.1 0.0 collective-permute-done.4
  30.1 0.3 slice_add_fusion.1
  30.4 3.0 %collective-permute-start.5 = (f32[128,1536]{1,0:T(8,128)S(1)}, f32[128,1536]{1,0:T(8,128)S(1)}, u32[]{:S(2)}, u32[]{:S(2)}) collective-permute-start(f32[128,1536]{1,0:T(8,128)S(1)} %get-tuple-element.13), channel_id=1, source_target_pairs={{0,2},{1,5},{2,0},{3,7},{4,6},{5,1},{6,4},{7,3},{8,10},{9,13},{10,... | collective-permute-start | bytes 2359304 | tf_op jit(solution)/shard_map/ppermute | solution.py:206
  33.4 0.0 collective-permute-done
  33.4 0.2 slice_add_fusion.3
  33.5 2.0 %collective-permute-start.1 = (f32[128,1024]{1,0:T(8,128)S(1)}, f32[128,1024]{1,0:T(8,128)S(1)}, u32[]{:S(2)}, u32[]{:S(2)}) collective-permute-start(f32[128,1024]{1,0:T(8,128)S(1)} %get-tuple-element.15), channel_id=1, source_target_pairs={{0,2},{1,5},{2,0},{3,7},{4,6},{5,1},{6,4},{7,3},{8,10},{9,13},{10,... | collective-permute-start | bytes 1572872 | tf_op jit(solution)/shard_map/ppermute | solution.py:206
  35.6 13.4 %collective-permute-done.1 = f32[128,1024]{1,0:T(8,128)S(1)} collective-permute-done((f32[128,1024]{1,0:T(8,128)S(1)}, f32[128,1024]{1,0:T(8,128)S(1)}, u32[]{:S(2)}, u32[]{:S(2)}) %collective-permute-start.1) | collective-permute-done | bytes 524320 | tf_op jit(solution)/shard_map/ppermute | solution.py:206
  49.0 0.1 slice_add_fusion.7
  49.0 2.2 %collective-permute-start.2 = (f32[64,1024]{1,0:T(8,128)S(1)}, f32[64,1024]{1,0:T(8,128)S(1)}, u32[]{:S(2)}, u32[]{:S(2)}) collective-permute-start(f32[64,1024]{1,0:T(8,128)S(1)} %get-tuple-element.19), channel_id=1, source_target_pairs={{0,4},{1,3},{2,6},{3,1},{4,0},{5,7},{6,2},{7,5},{8,12},{9,11},{10,... | collective-permute-start | bytes 786440 | tf_op jit(solution)/shard_map/ppermute | solution.py:206
  51.2 0.0 collective-permute-done.5
  51.2 0.1 slice_add_fusion.5
  51.3 0.1 collective-permute-start.6
  51.4 0.1 broadcast_in_dim.30
  51.5 0.1 eq.31
  51.6 4.0 %collective-permute-done.2 = f32[64,1024]{1,0:T(8,128)S(1)} collective-permute-done((f32[64,1024]{1,0:T(8,128)S(1)}, f32[64,1024]{1,0:T(8,128)S(1)}, u32[]{:S(2)}, u32[]{:S(2)}) %collective-permute-start.2) | collective-permute-done | bytes 262176 | tf_op jit(solution)/shard_map/ppermute | solution.py:206
  55.6 3.1 %collective-permute-start.3 = (f32[32,1024]{1,0:T(8,128)S(1)}, f32[32,1024]{1,0:T(8,128)S(1)}, u32[]{:S(2)}, u32[]{:S(2)}) collective-permute-start(f32[32,1024]{1,0:T(8,128)S(1)} %slice_add_fusion.10), channel_id=1, source_target_pairs={{0,8},{1,9},{2,10},{3,11},{4,12},{5,13},{6,14},{7,15},{8,0},{9,1},... | collective-permute-start | bytes 393224 | tf_op jit(solution)/shard_map/ppermute | solution.py:206
  58.7 4.8 %collective-permute-done.6 = f32[64,1536]{1,0:T(8,128)S(1)} collective-permute-done((f32[64,1536]{1,0:T(8,128)S(1)}, f32[64,1536]{1,0:T(8,128)S(1)}, u32[]{:S(2)}, u32[]{:S(2)}) %collective-permute-start.6) | collective-permute-done | bytes 393248 | tf_op jit(solution)/shard_map/ppermute | solution.py:206
  63.5 0.0 copy-start
  63.5 1.3 %collective-permute-start.7 = (f32[32,1536]{1,0:T(8,128)S(1)}, f32[32,1536]{1,0:T(8,128)S(1)}, u32[]{:S(2)}, u32[]{:S(2)}) collective-permute-start(f32[32,1536]{1,0:T(8,128)S(1)} %slice_add_fusion.8), channel_id=1, source_target_pairs={{0,8},{1,9},{2,10},{3,11},{4,12},{5,13},{6,14},{7,15},{8,0},{9,1},... | collective-permute-start | bytes 589832 | tf_op jit(solution)/shard_map/ppermute | solution.py:206
  64.8 0.0 collective-permute-done.3
  64.8 0.1 reshape.70
  64.9 0.2 fusion.8
  65.2 7.1 %collective-permute-done.7 = f32[32,1536]{1,0:T(8,128)S(1)} collective-permute-done((f32[32,1536]{1,0:T(8,128)S(1)}, f32[32,1536]{1,0:T(8,128)S(1)}, u32[]{:S(2)}, u32[]{:S(2)}) %collective-permute-start.7) | collective-permute-done | bytes 196640 | tf_op jit(solution)/shard_map/ppermute | solution.py:206
  72.3 0.1 reshape.71
  72.5 0.3 fusion.7
  72.8 1.1 %fusion.10 = (f32[64]{0:T(128)S(1)}, f32[32,64]{1,0:T(8,128)}) fusion(s32[1280]{0:T(1024)S(1)} %eq.31, f32[32,768]{1,0:T(8,128)S(1)} %bitcast.8, f32[32,512]{1,0:T(8,128)S(1)} %bitcast.9), kind=kOutput, calls=%fused_computation.42 | convolution fusion | flops 31582144 | bytes 177408 | tf_op jit(solution)/shard_map/dot_general | solution.py:218
  73.9 0.1 reduce_sum.37
  74.0 0.1 reduce_sum.38
  74.1 0.1 collective-permute-start.8
  74.2 1.1 %collective-permute-done.8 = f32[16]{0:T(128)S(1)} collective-permute-done((f32[16]{0:T(128)S(1)}, f32[16]{0:T(128)S(1)}, u32[]{:S(2)}, u32[]{:S(2)}) %collective-permute-start.8) | collective-permute-done | bytes 96 | tf_op jit(solution)/shard_map/ppermute | solution.py:221
  75.3 1.7 %collective-permute-start.9 = (f32[16]{0:T(128)S(1)}, f32[16]{0:T(128)S(1)}, u32[]{:S(2)}, u32[]{:S(2)}) collective-permute-start(f32[16]{0:T(128)S(1)} %add.86), channel_id=1, source_target_pairs={{0,2},{1,5},{2,0},{3,7},{4,6},{5,1},{6,4},{7,3},{8,10},{9,13},{10,... | collective-permute-start | bytes 200 | tf_op jit(solution)/shard_map/ppermute | solution.py:221
  76.9 1.9 %collective-permute-done.9 = f32[16]{0:T(128)S(1)} collective-permute-done((f32[16]{0:T(128)S(1)}, f32[16]{0:T(128)S(1)}, u32[]{:S(2)}, u32[]{:S(2)}) %collective-permute-start.9) | collective-permute-done | bytes 96 | tf_op jit(solution)/shard_map/ppermute | solution.py:221
  78.8 0.4 collective-permute-start.10
  79.2 3.1 %collective-permute-done.10 = f32[16]{0:T(128)S(1)} collective-permute-done((f32[16]{0:T(128)S(1)}, f32[16]{0:T(128)S(1)}, u32[]{:S(2)}, u32[]{:S(2)}) %collective-permute-start.10) | collective-permute-done | bytes 96 | tf_op jit(solution)/shard_map/ppermute | solution.py:221
  82.4 1.8 %collective-permute-start.11 = (f32[16]{0:T(128)S(1)}, f32[16]{0:T(128)S(1)}, u32[]{:S(2)}, u32[]{:S(2)}) collective-permute-start(f32[16]{0:T(128)S(1)} %add.88), channel_id=1, source_target_pairs={{0,8},{1,9},{2,10},{3,11},{4,12},{5,13},{6,14},{7,15},{8,0},{9,1},... | collective-permute-start | bytes 200 | tf_op jit(solution)/shard_map/ppermute | solution.py:221
  84.2 2.7 %collective-permute-done.11 = f32[16]{0:T(128)S(1)} collective-permute-done((f32[16]{0:T(128)S(1)}, f32[16]{0:T(128)S(1)}, u32[]{:S(2)}, u32[]{:S(2)}) %collective-permute-start.11) | collective-permute-done | bytes 96 | tf_op jit(solution)/shard_map/ppermute | solution.py:221
  86.8 0.0 copy-done
  86.8 0.5 rsqrt_multiply_fusion
  (12 shorter events, 0.2 us)
Async XLA Ops:
  19.0 11.2 %collective-permute-start.4 = (f32[256,1536]{1,0:T(8,128)S(1)}, f32[256,1536]{1,0:T(8,128)S(1)}, u32[]{:S(2)}, u32[]{:S(2)}) collective-permute-start(f32[256,1536]{1,0:T(8,128)S(1)} %get-tuple-element.9), channel_id=1, source_target_pairs={{0,1},{1,0},{2,3},{3,2},{4,5},{5,4},{6,7},{7,6},{8,9},{9,8},{10,11... | collective-permute-start | bytes 4718600 | tf_op jit(solution)/shard_map/ppermute | solution.py:206
  30.0 3.4 %collective-permute-start = (f32[256,1024]{1,0:T(8,128)S(1)}, f32[256,1024]{1,0:T(8,128)S(1)}, u32[]{:S(2)}, u32[]{:S(2)}) collective-permute-start(f32[256,1024]{1,0:T(8,128)S(1)} %get-tuple-element.7), channel_id=1, source_target_pairs={{0,1},{1,0},{2,3},{3,2},{4,5},{5,4},{6,7},{7,6},{8,9},{9,8},{10,11... | collective-permute-start | bytes 3145736 | tf_op jit(solution)/shard_map/ppermute | solution.py:206
  30.4 20.8 %collective-permute-start.5 = (f32[128,1536]{1,0:T(8,128)S(1)}, f32[128,1536]{1,0:T(8,128)S(1)}, u32[]{:S(2)}, u32[]{:S(2)}) collective-permute-start(f32[128,1536]{1,0:T(8,128)S(1)} %get-tuple-element.13), channel_id=1, source_target_pairs={{0,2},{1,5},{2,0},{3,7},{4,6},{5,1},{6,4},{7,3},{8,10},{9,13},{10,... | collective-permute-start | bytes 2359304 | tf_op jit(solution)/shard_map/ppermute | solution.py:206
  33.5 15.4 %collective-permute-start.1 = (f32[128,1024]{1,0:T(8,128)S(1)}, f32[128,1024]{1,0:T(8,128)S(1)}, u32[]{:S(2)}, u32[]{:S(2)}) collective-permute-start(f32[128,1024]{1,0:T(8,128)S(1)} %get-tuple-element.15), channel_id=1, source_target_pairs={{0,2},{1,5},{2,0},{3,7},{4,6},{5,1},{6,4},{7,3},{8,10},{9,13},{10,... | collective-permute-start | bytes 1572872 | tf_op jit(solution)/shard_map/ppermute | solution.py:206
  49.0 6.5 %collective-permute-start.2 = (f32[64,1024]{1,0:T(8,128)S(1)}, f32[64,1024]{1,0:T(8,128)S(1)}, u32[]{:S(2)}, u32[]{:S(2)}) collective-permute-start(f32[64,1024]{1,0:T(8,128)S(1)} %get-tuple-element.19), channel_id=1, source_target_pairs={{0,4},{1,3},{2,6},{3,1},{4,0},{5,7},{6,2},{7,5},{8,12},{9,11},{10,... | collective-permute-start | bytes 786440 | tf_op jit(solution)/shard_map/ppermute | solution.py:206
  51.3 12.2 %collective-permute-start.6 = (f32[64,1536]{1,0:T(8,128)S(1)}, f32[64,1536]{1,0:T(8,128)S(1)}, u32[]{:S(2)}, u32[]{:S(2)}) collective-permute-start(f32[64,1536]{1,0:T(8,128)S(1)} %get-tuple-element.17), channel_id=1, source_target_pairs={{0,4},{1,3},{2,6},{3,1},{4,0},{5,7},{6,2},{7,5},{8,12},{9,11},{10,... | collective-permute-start | bytes 1179656 | tf_op jit(solution)/shard_map/ppermute | solution.py:206
  55.6 9.2 %collective-permute-start.3 = (f32[32,1024]{1,0:T(8,128)S(1)}, f32[32,1024]{1,0:T(8,128)S(1)}, u32[]{:S(2)}, u32[]{:S(2)}) collective-permute-start(f32[32,1024]{1,0:T(8,128)S(1)} %slice_add_fusion.10), channel_id=1, source_target_pairs={{0,8},{1,9},{2,10},{3,11},{4,12},{5,13},{6,14},{7,15},{8,0},{9,1},... | collective-permute-start | bytes 393224 | tf_op jit(solution)/shard_map/ppermute | solution.py:206
  63.5 23.3 %copy-start = (s32[16]{0:T(128)S(1)}, s32[16]{0:T(128)}, u32[]{:S(2)}) copy-start(s32[16]{0:T(128)} %param.11) | copy-start | bytes 196
  63.5 8.8 %collective-permute-start.7 = (f32[32,1536]{1,0:T(8,128)S(1)}, f32[32,1536]{1,0:T(8,128)S(1)}, u32[]{:S(2)}, u32[]{:S(2)}) collective-permute-start(f32[32,1536]{1,0:T(8,128)S(1)} %slice_add_fusion.8), channel_id=1, source_target_pairs={{0,8},{1,9},{2,10},{3,11},{4,12},{5,13},{6,14},{7,15},{8,0},{9,1},... | collective-permute-start | bytes 589832 | tf_op jit(solution)/shard_map/ppermute | solution.py:206
  74.1 1.2 %collective-permute-start.8 = (f32[16]{0:T(128)S(1)}, f32[16]{0:T(128)S(1)}, u32[]{:S(2)}, u32[]{:S(2)}) collective-permute-start(f32[16]{0:T(128)S(1)} %reduce_sum.38), channel_id=1, source_target_pairs={{0,1},{1,0},{2,3},{3,2},{4,5},{5,4},{6,7},{7,6},{8,9},{9,8},{10,11... | collective-permute-start | bytes 200 | tf_op jit(solution)/shard_map/ppermute | solution.py:221
  75.3 3.5 %collective-permute-start.9 = (f32[16]{0:T(128)S(1)}, f32[16]{0:T(128)S(1)}, u32[]{:S(2)}, u32[]{:S(2)}) collective-permute-start(f32[16]{0:T(128)S(1)} %add.86), channel_id=1, source_target_pairs={{0,2},{1,5},{2,0},{3,7},{4,6},{5,1},{6,4},{7,3},{8,10},{9,13},{10,... | collective-permute-start | bytes 200 | tf_op jit(solution)/shard_map/ppermute | solution.py:221
  78.8 3.5 %collective-permute-start.10 = (f32[16]{0:T(128)S(1)}, f32[16]{0:T(128)S(1)}, u32[]{:S(2)}, u32[]{:S(2)}) collective-permute-start(f32[16]{0:T(128)S(1)} %add.87), channel_id=1, source_target_pairs={{0,4},{1,3},{2,6},{3,1},{4,0},{5,7},{6,2},{7,5},{8,12},{9,11},{10,... | collective-permute-start | bytes 200 | tf_op jit(solution)/shard_map/ppermute | solution.py:221
  82.4 4.4 %collective-permute-start.11 = (f32[16]{0:T(128)S(1)}, f32[16]{0:T(128)S(1)}, u32[]{:S(2)}, u32[]{:S(2)}) collective-permute-start(f32[16]{0:T(128)S(1)} %add.88), channel_id=1, source_target_pairs={{0,8},{1,9},{2,10},{3,11},{4,12},{5,13},{6,14},{7,15},{8,0},{9,1},... | collective-permute-start | bytes 200 | tf_op jit(solution)/shard_map/ppermute | solution.py:221
